TPU v7x, 512 devices: a whole 4x8x8 slice. The times are simulated.
512 devices in a mesh: delay: 16 (over y, core), row: 32 (over z, x).
Axes of the slice: x: 4, y: 8, z: 8, core: 2. Of those that a mesh axis runs over, the one named last changes fastest.
Arguments:
- incident: bfloat16 [64, 4096], P(None, 'row'), may hold values from -12 to 12
- onset: int32 [64], replicated, may hold values from 0 to 2
- beta: float32 [4096], P('delay'), may hold values from 0.05 to 0.5
- inverse_block: bfloat16 [4096, 4096], P('row', 'delay'), may hold values from -0.0625 to 0.0625
- delay_blocks: bfloat16 [16, 4096, 4096], P('delay', None, 'row'), may hold values from -0.09375 to 0.09375
- history_sum: float32 [16, 64, 4096], P('delay', None, 'row'), may hold values from -12 to 12
Outputs:
- currents: bfloat16 [3, 64, 4096], P(None, None, 'delay')
- carried: float32 [16, 64, 4096], P('delay', None, 'row')
All inputs are finite; a program needn't handle non-finite values.
Results may differ from a plain program's by a relative error of at most 0.0056.
Values may be sent and summed in bfloat16 or wider, within the bound.
A program may use at most 64 MiB of HBM per device.

v0:
```python
import jax
import jax.numpy as jnp
from jax import lax
from jax.sharding import PartitionSpec as P

STEPS = 3


def broadcast(value, axis, root):
    return lax.dynamic_index_in_dim(lax.all_gather(value, axis), root, 0, keepdims=False)


def in_blocks(value, dim, devices):
    dims = value.shape
    blocks = value.reshape(*dims[:dim], devices, dims[dim] // devices, *dims[dim + 1 :])
    return jnp.moveaxis(blocks, dim, 0)


def sent_and_summed(value, axis, dim):
    devices = lax.axis_size(axis)
    blocks = lax.all_to_all(in_blocks(value, dim, devices), axis, 0, 0, tiled=True)
    return jnp.sum(blocks, axis=0)


def copy_for_each(value, axis):
    copies = jnp.broadcast_to(value, (lax.axis_size(axis), *value.shape))
    return lax.all_to_all(copies, axis, split_axis=0, concat_axis=0, tiled=True)


def joined_along(blocks, dim):
    blocks = jnp.moveaxis(blocks, 0, dim)
    dims = blocks.shape
    return blocks.reshape(*dims[:dim], dims[dim] * dims[dim + 1], *dims[dim + 2 :])


def gathered_copies(value, axis, dim):
    blocks = copy_for_each(value, axis)
    return joined_along(blocks, dim)


def passed_along(value, axis, by):
    devices = lax.axis_size(axis)
    pairs = [(i, i + by) for i in range(devices) if 0 <= i + by < devices]
    return lax.ppermute(value, axis, pairs)


def per_device(incident, onset, beta, inverse_block, delay_blocks, history_sum):
    future = history_sum[0]
    matrix = delay_blocks[0]
    incident_wide = incident.astype(jnp.float32)
    outputs = []
    for step_index in range(STEPS):
        offset_time = (step_index - onset).astype(jnp.float32)
        envelope = jnp.where(offset_time >= 0.0, jnp.exp(-((offset_time - 1.0) ** 2) / 4.0), 0.0)
        residual = (incident_wide * envelope[:, None] - future).astype(jnp.bfloat16)
        residual = broadcast(residual, "delay", 0)
        partial_sum = jnp.dot(residual, inverse_block, preferred_element_type=jnp.float32)
        solved = sent_and_summed(partial_sum, "row", 0)
        current = (solved / (1.0 + beta[None, :] * solved * solved)).astype(jnp.bfloat16)
        own_block = gathered_copies(current, "row", 0)
        gathered = lax.all_gather(own_block, "delay", axis=1, tiled=True)
        outputs.append(own_block)
        passed = passed_along(future, "delay", -1)
        future = passed + jnp.dot(gathered, matrix, preferred_element_type=jnp.float32)
    return (jnp.stack(outputs), future[None])


def solution(mesh):
    placed = (
        P(None, "row"),
        P(),
        P("delay"),
        P("row", "delay"),
        P("delay", None, "row"),
        P("delay", None, "row"),
    )
    return jax.shard_map(
        per_device,
        mesh=mesh,
        in_specs=placed,
        out_specs=(P(None, None, "delay"), P("delay", None, "row")),
        check_vma=False,
    )
```

profile of v0, /device:TPU:1, one launch (start us, length us, event | category | flops | bytes accessed | tf_op | source)
XLA Modules:
  0.0 199.1 jit_solution(9493592428893358727)
XLA Ops:
  0.6 0.0 copy-start
  0.6 0.8 compare_select_fusion.1
  1.4 0.9 fusion.12
  2.3 0.0 copy-start.1
  2.3 21.7 %all-gather = bf16[1024,128]{1,0:T(8,128)(2,1)S(1)} all-gather(bf16[64,128]{1,0:T(8,128)(2,1)S(1)} %fusion.12), channel_id=2, replica_groups=mesh['delay'=16,'row'=32] {'delay'}, dimensions={0}, use_global_device_ids=true | all-gather | bytes 278528 | tf_op jit(solution)/shard_map/all_gather | solution.py:10
  24.0 0.0 copy-done.1
  24.0 0.1 fusion.9
  24.1 0.1 copy.14
  24.2 19.6 %all_to_all.30 = f32[32,2,256]{2,1,0:T(2,128)S(1)} all-to-all(f32[32,2,256]{2,1,0:T(2,128)S(1)} %copy.14), channel_id=1, replica_groups=mesh['delay'=16,'row'=32] {'row'}, dimensions={0} | all-to-all | bytes 131072 | tf_op jit(solution)/shard_map/all_to_all | solution.py:21
  43.8 0.0 copy-start.4
  43.8 0.6 copy-done.4
  44.5 0.6 broadcast_in_dim.22
  45.1 0.0 copy-start.3
  45.1 4.0 %all-to-all-start.1 = ((bf16[32,2,256]{2,1,0:T(2,128)(2,1)}), bf16[32,2,256]{2,1,0:T(2,128)(2,1)S(1)}, u32[]{:S(2)}, u32[]{:S(2)}) async-start(bf16[32,2,256]{2,1,0:T(2,128)(2,1)} %broadcast_in_dim.22), calls=%async_computation.1 | async-start | bytes 65536 | tf_op jit(solution)/shard_map/all_to_all | solution.py:27
  49.1 0.0 copy-done.3
  49.1 3.5 %collective-permute-start = (f32[64,128]{1,0:T(8,128)S(1)}, f32[64,128]{1,0:T(8,128)S(1)}, u32[]{:S(2)}, u32[]{:S(2)}) collective-permute-start(f32[64,128]{1,0:T(8,128)S(1)} %bitcast.29), channel_id=1, source_target_pairs={{32,0},{64,32},{96,64},{128,96},{160,128},{192,160},{224,192},{256... | collective-permute-start | bytes 98312 | tf_op jit(solution)/shard_map/ppermute | solution.py:44
  52.6 5.1 %all-to-all-done.1 = bf16[32,2,256]{2,1,0:T(2,128)(2,1)S(1)} async-done(((bf16[32,2,256]{2,1,0:T(2,128)(2,1)}), bf16[32,2,256]{2,1,0:T(2,128)(2,1)S(1)}, u32[]{:S(2)}, u32[]{:S(2)}) %all-to-all-start.1) | async-done | bytes 32800 | tf_op jit(solution)/shard_map/all_to_all | solution.py:27
  57.7 0.0 copy-start.2
  57.8 18.9 %all_gather.29 = bf16[64,4096]{1,0:T(8,128)(2,1)S(1)} all-gather(bf16[64,256]{1,0:T(8,128)(2,1)S(1)} %reshape.26), channel_id=1, replica_groups=mesh['delay'=16,'row'=32] {'delay'}, dimensions={1}, use_global_device_ids=true | all-gather | bytes 557056 | tf_op jit(solution)/shard_map/all_gather | solution.py:61
  76.7 0.0 collective-permute-done
  76.7 0.0 copy-done
  76.7 0.0 copy-done.2
  76.7 0.3 fusion.14
  77.0 16.0 %all-gather.1 = bf16[1024,128]{1,0:T(8,128)(2,1)S(1)} all-gather(bf16[64,128]{1,0:T(8,128)(2,1)S(1)} %get-tuple-element.7), channel_id=3, replica_groups=mesh['delay'=16,'row'=32] {'delay'}, dimensions={0}, use_global_device_ids=true | all-gather | bytes 278528 | tf_op jit(solution)/shard_map/all_gather | solution.py:10
  93.1 0.1 fusion.7
  93.2 0.1 copy.16
  93.3 11.8 %all_to_all.31 = f32[32,2,256]{2,1,0:T(2,128)S(1)} all-to-all(f32[32,2,256]{2,1,0:T(2,128)S(1)} %copy.16), channel_id=1, replica_groups=mesh['delay'=16,'row'=32] {'row'}, dimensions={0} | all-to-all | bytes 131072 | tf_op jit(solution)/shard_map/all_to_all | solution.py:21
  105.2 0.6 broadcast_in_dim.23
  105.8 3.9 %all-to-all-start.3 = ((bf16[32,2,256]{2,1,0:T(2,128)(2,1)}), bf16[32,2,256]{2,1,0:T(2,128)(2,1)S(1)}, u32[]{:S(2)}, u32[]{:S(2)}) async-start(bf16[32,2,256]{2,1,0:T(2,128)(2,1)} %broadcast_in_dim.23), calls=%async_computation.3 | async-start | bytes 65536 | tf_op jit(solution)/shard_map/all_to_all | solution.py:27
  109.7 3.3 %collective-permute-start.1 = (f32[64,128]{1,0:T(8,128)S(1)}, f32[64,128]{1,0:T(8,128)S(1)}, u32[]{:S(2)}, u32[]{:S(2)}) collective-permute-start(f32[64,128]{1,0:T(8,128)S(1)} %get-tuple-element.8), channel_id=1, source_target_pairs={{32,0},{64,32},{96,64},{128,96},{160,128},{192,160},{224,192},{256... | collective-permute-start | bytes 98312 | tf_op jit(solution)/shard_map/ppermute | solution.py:44
  113.0 5.3 %all-to-all-done.3 = bf16[32,2,256]{2,1,0:T(2,128)(2,1)S(1)} async-done(((bf16[32,2,256]{2,1,0:T(2,128)(2,1)}), bf16[32,2,256]{2,1,0:T(2,128)(2,1)S(1)}, u32[]{:S(2)}, u32[]{:S(2)}) %all-to-all-start.3) | async-done | bytes 32800 | tf_op jit(solution)/shard_map/all_to_all | solution.py:27
  118.3 18.7 %all_gather.32 = bf16[64,4096]{1,0:T(8,128)(2,1)S(1)} all-gather(bf16[64,256]{1,0:T(8,128)(2,1)S(1)} %reshape.27), channel_id=1, replica_groups=mesh['delay'=16,'row'=32] {'delay'}, dimensions={1}, use_global_device_ids=true | all-gather | bytes 557056 | tf_op jit(solution)/shard_map/all_gather | solution.py:61
  137.0 0.3 fusion.2
  137.4 0.0 collective-permute-done.1
  137.4 0.1 fusion.16
  137.5 16.0 %all-gather.2 = bf16[1024,128]{1,0:T(8,128)(2,1)S(1)} all-gather(bf16[64,128]{1,0:T(8,128)(2,1)S(1)} %get-tuple-element.2), channel_id=4, replica_groups=mesh['delay'=16,'row'=32] {'delay'}, dimensions={0}, use_global_device_ids=true | all-gather | bytes 278528 | tf_op jit(solution)/shard_map/all_gather | solution.py:10
  153.5 0.1 fusion.5
  153.6 0.1 copy.18
  153.7 11.8 %all_to_all.32 = f32[32,2,256]{2,1,0:T(2,128)S(1)} all-to-all(f32[32,2,256]{2,1,0:T(2,128)S(1)} %copy.18), channel_id=1, replica_groups=mesh['delay'=16,'row'=32] {'row'}, dimensions={0} | all-to-all | bytes 131072 | tf_op jit(solution)/shard_map/all_to_all | solution.py:21
  165.6 0.6 broadcast_in_dim.24
  166.2 3.9 %all-to-all-start.5 = ((bf16[32,2,256]{2,1,0:T(2,128)(2,1)}), bf16[32,2,256]{2,1,0:T(2,128)(2,1)S(1)}, u32[]{:S(2)}, u32[]{:S(2)}) async-start(bf16[32,2,256]{2,1,0:T(2,128)(2,1)} %broadcast_in_dim.24), calls=%async_computation.5 | async-start | bytes 65536 | tf_op jit(solution)/shard_map/all_to_all | solution.py:27
  170.1 3.3 %collective-permute-start.2 = (f32[64,128]{1,0:T(8,128)S(1)}, f32[64,128]{1,0:T(8,128)S(1)}, u32[]{:S(2)}, u32[]{:S(2)}) collective-permute-start(f32[64,128]{1,0:T(8,128)S(1)} %get-tuple-element.3), channel_id=1, source_target_pairs={{32,0},{64,32},{96,64},{128,96},{160,128},{192,160},{224,192},{256... | collective-permute-start | bytes 98312 | tf_op jit(solution)/shard_map/ppermute | solution.py:44
  173.4 5.3 %all-to-all-done.5 = bf16[32,2,256]{2,1,0:T(2,128)(2,1)S(1)} async-done(((bf16[32,2,256]{2,1,0:T(2,128)(2,1)}), bf16[32,2,256]{2,1,0:T(2,128)(2,1)S(1)}, u32[]{:S(2)}, u32[]{:S(2)}) %all-to-all-start.5) | async-done | bytes 32800 | tf_op jit(solution)/shard_map/all_to_all | solution.py:27
  178.7 18.7 %all_gather.35 = bf16[64,4096]{1,0:T(8,128)(2,1)S(1)} all-gather(bf16[64,256]{1,0:T(8,128)(2,1)S(1)} %reshape.28), channel_id=1, replica_groups=mesh['delay'=16,'row'=32] {'delay'}, dimensions={1}, use_global_device_ids=true | all-gather | bytes 557056 | tf_op jit(solution)/shard_map/all_gather | solution.py:61
  197.5 0.3 fusion
  197.8 0.7 pad_maximum_fusion
  198.5 0.0 collective-permute-done.2
  198.5 0.6 add_bitcast_fusion
  (15 shorter events, 0.3 us)
Async XLA Ops:
  0.6 76.0 %copy-start = (bf16[1,4096,128]{2,1,0:T(8,128)(2,1)S(1)}, bf16[1,4096,128]{2,1,0:T(8,128)(2,1)}, u32[]{:S(2)}) copy-start(bf16[1,4096,128]{2,1,0:T(8,128)(2,1)} %param.10) | copy-start | bytes 3145732
  2.3 21.7 %copy-start.1 = (bf16[128,256]{1,0:T(8,128)(2,1)S(1)}, bf16[128,256]{1,0:T(8,128)(2,1)}, u32[]{:S(2)}) copy-start(bf16[128,256]{1,0:T(8,128)(2,1)} %param.9) | copy-start | bytes 196612
  43.8 0.7 copy-start.4
  45.1 4.0 %copy-start.3 = (f32[1,64,128]{2,1,0:T(8,128)S(1)}, f32[1,64,128]{2,1,0:T(8,128)}, u32[]{:S(2)}) copy-start(f32[1,64,128]{2,1,0:T(8,128)} %param.11) | copy-start | bytes 98308
  45.1 12.6 %all-to-all-start.1 = ((bf16[32,2,256]{2,1,0:T(2,128)(2,1)}), bf16[32,2,256]{2,1,0:T(2,128)(2,1)S(1)}, u32[]{:S(2)}, u32[]{:S(2)}) async-start(bf16[32,2,256]{2,1,0:T(2,128)(2,1)} %broadcast_in_dim.22), calls=%async_computation.1 | async-start | bytes 65536 | tf_op jit(solution)/shard_map/all_to_all | solution.py:27
  49.1 27.6 %collective-permute-start = (f32[64,128]{1,0:T(8,128)S(1)}, f32[64,128]{1,0:T(8,128)S(1)}, u32[]{:S(2)}, u32[]{:S(2)}) collective-permute-start(f32[64,128]{1,0:T(8,128)S(1)} %bitcast.29), channel_id=1, source_target_pairs={{32,0},{64,32},{96,64},{128,96},{160,128},{192,160},{224,192},{256... | collective-permute-start | bytes 98312 | tf_op jit(solution)/shard_map/ppermute | solution.py:44
  57.7 18.9 %copy-start.2 = (bf16[64,128]{1,0:T(8,128)(2,1)S(1)}, bf16[64,128]{1,0:T(8,128)(2,1)}, u32[]{:S(2)}) copy-start(bf16[64,128]{1,0:T(8,128)(2,1)} %param.6) | copy-start | bytes 49156
  105.8 12.5 %all-to-all-start.3 = ((bf16[32,2,256]{2,1,0:T(2,128)(2,1)}), bf16[32,2,256]{2,1,0:T(2,128)(2,1)S(1)}, u32[]{:S(2)}, u32[]{:S(2)}) async-start(bf16[32,2,256]{2,1,0:T(2,128)(2,1)} %broadcast_in_dim.23), calls=%async_computation.3 | async-start | bytes 65536 | tf_op jit(solution)/shard_map/all_to_all | solution.py:27
  109.7 27.7 %collective-permute-start.1 = (f32[64,128]{1,0:T(8,128)S(1)}, f32[64,128]{1,0:T(8,128)S(1)}, u32[]{:S(2)}, u32[]{:S(2)}) collective-permute-start(f32[64,128]{1,0:T(8,128)S(1)} %get-tuple-element.8), channel_id=1, source_target_pairs={{32,0},{64,32},{96,64},{128,96},{160,128},{192,160},{224,192},{256... | collective-permute-start | bytes 98312 | tf_op jit(solution)/shard_map/ppermute | solution.py:44
  166.2 12.5 %all-to-all-start.5 = ((bf16[32,2,256]{2,1,0:T(2,128)(2,1)}), bf16[32,2,256]{2,1,0:T(2,128)(2,1)S(1)}, u32[]{:S(2)}, u32[]{:S(2)}) async-start(bf16[32,2,256]{2,1,0:T(2,128)(2,1)} %broadcast_in_dim.24), calls=%async_computation.5 | async-start | bytes 65536 | tf_op jit(solution)/shard_map/all_to_all | solution.py:27
  170.1 28.4 %collective-permute-start.2 = (f32[64,128]{1,0:T(8,128)S(1)}, f32[64,128]{1,0:T(8,128)S(1)}, u32[]{:S(2)}, u32[]{:S(2)}) collective-permute-start(f32[64,128]{1,0:T(8,128)S(1)} %get-tuple-element.3), channel_id=1, source_target_pairs={{32,0},{64,32},{96,64},{128,96},{160,128},{192,160},{224,192},{256... | collective-permute-start | bytes 98312 | tf_op jit(solution)/shard_map/ppermute | solution.py:44
where the time goes:
time: 200 us; the launch traced here: 199 us
  blocking collectives  153 us (76%)
  starting transfers between devices  21.8 us (11%)
  waiting for transfers between devices  15.7 us (8%)
  other arithmetic  3.13 us (2%)
  local copies, waits for them, and re-layouts  2.87 us (1%)
    all_gather x3, blocking collectives, per_device(): gathered = lax.all_gather(own_block, 'delay', axis=1, tiled=True)  56.4 us
    all_gather x3, blocking collectives, broadcast(): lax.all_gather(value, axis)  53.8 us
    all_to_all x3, blocking collectives, sent_and_summed(): lax.all_to_all(in_blocks(value, dim, devices), axis, 0, 0, tiled=True)  43.3 us
    all_to_all x3, waiting for transfers between devices, copy_for_each(): return lax.all_to_all(copies, axis, split_axis=0, concat_axis=0, tiled=True)  15.7 us
    all_to_all x3, starting transfers between devices, copy_for_each(): return lax.all_to_all(copies, axis, split_axis=0, concat_axis=0, tiled=True)  11.7 us
    ppermute x3, starting transfers between devices, passed_along(): return lax.ppermute(value, axis, pairs)  10.1 us
  transfers between devices with their start and end apart: 6, of which 3 were waited for; matrix products, arithmetic and copies ran while one was open for 1% of the time, Pallas kernels for 0%

commit v1 on v0

--- a/solution.py
+++ b/solution.py
@@ -58,7 +58,9 @@
         solved = sent_and_summed(partial_sum, "row", 0)
         current = (solved / (1.0 + beta[None, :] * solved * solved)).astype(jnp.bfloat16)
         own_block = gathered_copies(current, "row", 0)
-        gathered = lax.all_gather(own_block, "delay", axis=1, tiled=True)
+        gathered = jnp.concatenate(
+            lax.all_to_all(jnp.stack([own_block] * lax.axis_size("delay")), "delay", 0, 0), axis=1
+        )
         outputs.append(own_block)
         passed = passed_along(future, "delay", -1)
         future = passed + jnp.dot(gathered, matrix, preferred_element_type=jnp.float32)

time: 200 us -> 215 us (1.075)
  waiting for transfers between devices: 15.7 us -> 45.2 us
  blocking collectives: 153 us -> 131 us
  starting transfers between devices: 21.8 us -> 28.1 us
    all_gather x3 -> x0, blocking collectives: 56.4 us -> none  [per_device(): gathered = lax.all_gather(own_block, 'delay', axis=1, tiled=True)]
    all_to_all x0 -> x3, blocking collectives: none -> 35.3 us  [copy_for_each(): return lax.all_to_all(copies, axis, split_axis=0, concat_axis=0, tiled=True)]
    all_to_all x3, waiting for transfers between devices: 15.7 us -> 45.2 us  [per_device(): lax.all_to_all(jnp.stack([own_block] * lax.axis_size('delay')), 'delay',...]
    all_to_all x3, starting transfers between devices: 11.7 us -> 22.1 us  [per_device(): lax.all_to_all(jnp.stack([own_block] * lax.axis_size('delay')), 'delay',...]
    ppermute x3, starting transfers between devices: 10.1 us -> 6.04 us  [passed_along(): return lax.ppermute(value, axis, pairs)]
    another operation x0 -> x3, local copies, waits for them, and re-layouts: none -> 2.57 us  [per_device(): jnp.stack([own_block] * lax.axis_size('delay'))]
where the time goes in v1:
time: 215 us; the launch traced here: 214 us
  blocking collectives  131 us (61%)
  waiting for transfers between devices  45.2 us (21%)
  starting transfers between devices  28.1 us (13%)
  local copies, waits for them, and re-layouts  4.34 us (2%)
  other arithmetic  3.13 us (1%)
    all_gather x3, blocking collectives, broadcast(): lax.all_gather(value, axis)  52.1 us
    all_to_all x3, waiting for transfers between devices, per_device(): lax.all_to_all(jnp.stack([own_block] * lax.axis_size('delay')), 'delay',...  45.2 us
    all_to_all x3, blocking collectives, sent_and_summed(): lax.all_to_all(in_blocks(value, dim, devices), axis, 0, 0, tiled=True)  43.3 us
    all_to_all x3, blocking collectives, copy_for_each(): return lax.all_to_all(copies, axis, split_axis=0, concat_axis=0, tiled=True)  35.3 us
    all_to_all x3, starting transfers between devices, per_device(): lax.all_to_all(jnp.stack([own_block] * lax.axis_size('delay')), 'delay',...  22.1 us
    ppermute x3, starting transfers between devices, passed_along(): return lax.ppermute(value, axis, pairs)  6.04 us
  transfers between devices with their start and end apart: 6, of which 3 were waited for; matrix products, arithmetic and copies ran while one was open for 1% of the time, Pallas kernels for 0%

profile of v1, /device:TPU:1, one launch (start us, length us, event | category | flops | bytes accessed | tf_op | source)
XLA Modules:
  0.0 213.6 jit_solution(750109058452023752)
XLA Ops:
  0.6 0.0 copy-start
  0.6 0.8 compare_select_fusion.1
  1.4 0.9 fusion.12
  2.3 0.0 copy-start.1
  2.3 21.7 %all-gather = bf16[1024,128]{1,0:T(8,128)(2,1)S(1)} all-gather(bf16[64,128]{1,0:T(8,128)(2,1)S(1)} %fusion.12), channel_id=2, replica_groups=mesh['delay'=16,'row'=32] {'delay'}, dimensions={0}, use_global_device_ids=true | all-gather | bytes 278528 | tf_op jit(solution)/shard_map/all_gather | solution.py:10
  24.0 0.0 copy-done.1
  24.0 0.1 fusion.9
  24.1 0.1 copy.14
  24.2 19.6 %all_to_all.45 = f32[32,2,256]{2,1,0:T(2,128)S(1)} all-to-all(f32[32,2,256]{2,1,0:T(2,128)S(1)} %copy.14), channel_id=1, replica_groups=mesh['delay'=16,'row'=32] {'row'}, dimensions={0} | all-to-all | bytes 131072 | tf_op jit(solution)/shard_map/all_to_all | solution.py:21
  43.8 0.0 copy-start.4
  43.8 0.6 copy-done.4
  44.5 11.8 %all_to_all.46 = bf16[32,2,256]{2,1,0:T(2,128)(2,1)S(1)} all-to-all(bf16[32,2,256]{2,1,0:T(2,128)(2,1)S(1)} %broadcast_in_dim.22), channel_id=1, replica_groups=mesh['delay'=16,'row'=32] {'row'}, dimensions={0} | all-to-all | bytes 65536 | tf_op jit(solution)/shard_map/all_to_all | solution.py:27
  56.3 0.9 stack.12
  57.2 0.0 copy-start.3
  57.2 7.2 %all-to-all-start.2 = ((bf16[16,64,256]{2,1,0:T(8,128)(2,1)}), bf16[16,64,256]{2,1,0:T(8,128)(2,1)S(1)}, u32[]{:S(2)}, u32[]{:S(2)}) async-start(bf16[16,64,256]{2,1,0:T(8,128)(2,1)} %stack.12), calls=%async_computation.2 | async-start | bytes 1048576 | tf_op jit(solution)/shard_map/all_to_all | solution.py:62
  64.3 0.0 copy-done.3
  64.3 2.0 collective-permute-start
  66.4 15.3 %all-to-all-done.2 = bf16[16,64,256]{2,1,0:T(8,128)(2,1)S(1)} async-done(((bf16[16,64,256]{2,1,0:T(8,128)(2,1)}), bf16[16,64,256]{2,1,0:T(8,128)(2,1)S(1)}, u32[]{:S(2)}, u32[]{:S(2)}) %all-to-all-start.2) | async-done | bytes 524320 | tf_op jit(solution)/shard_map/all_to_all | solution.py:62
  81.7 0.0 copy-start.2
  81.7 0.0 collective-permute-done
  81.7 0.0 copy-done
  81.7 0.7 copy-done.2
  82.4 0.3 fusion.14
  82.7 15.2 %all-gather.1 = bf16[1024,128]{1,0:T(8,128)(2,1)S(1)} all-gather(bf16[64,128]{1,0:T(8,128)(2,1)S(1)} %get-tuple-element.7), channel_id=3, replica_groups=mesh['delay'=16,'row'=32] {'delay'}, dimensions={0}, use_global_device_ids=true | all-gather | bytes 278528 | tf_op jit(solution)/shard_map/all_gather | solution.py:10
  97.9 0.1 fusion.7
  98.0 0.1 copy.17
  98.1 11.9 %all_to_all.47 = f32[32,2,256]{2,1,0:T(2,128)S(1)} all-to-all(f32[32,2,256]{2,1,0:T(2,128)S(1)} %copy.17), channel_id=1, replica_groups=mesh['delay'=16,'row'=32] {'row'}, dimensions={0} | all-to-all | bytes 131072 | tf_op jit(solution)/shard_map/all_to_all | solution.py:21
  110.0 11.8 %all_to_all.48 = bf16[32,2,256]{2,1,0:T(2,128)(2,1)S(1)} all-to-all(bf16[32,2,256]{2,1,0:T(2,128)(2,1)S(1)} %broadcast_in_dim.23), channel_id=1, replica_groups=mesh['delay'=16,'row'=32] {'row'}, dimensions={0} | all-to-all | bytes 65536 | tf_op jit(solution)/shard_map/all_to_all | solution.py:27
  121.8 0.9 stack.13
  122.7 7.4 %all-to-all-start.5 = ((bf16[16,64,256]{2,1,0:T(8,128)(2,1)}), bf16[16,64,256]{2,1,0:T(8,128)(2,1)S(1)}, u32[]{:S(2)}, u32[]{:S(2)}) async-start(bf16[16,64,256]{2,1,0:T(8,128)(2,1)} %stack.13), calls=%async_computation.5 | async-start | bytes 1048576 | tf_op jit(solution)/shard_map/all_to_all | solution.py:62
  130.1 2.0 collective-permute-start.1
  132.1 15.3 %all-to-all-done.5 = bf16[16,64,256]{2,1,0:T(8,128)(2,1)S(1)} async-done(((bf16[16,64,256]{2,1,0:T(8,128)(2,1)}), bf16[16,64,256]{2,1,0:T(8,128)(2,1)S(1)}, u32[]{:S(2)}, u32[]{:S(2)}) %all-to-all-start.5) | async-done | bytes 524320 | tf_op jit(solution)/shard_map/all_to_all | solution.py:62
  147.5 0.3 fusion.2
  147.8 0.0 collective-permute-done.1
  147.8 0.1 fusion.16
  147.9 15.2 %all-gather.2 = bf16[1024,128]{1,0:T(8,128)(2,1)S(1)} all-gather(bf16[64,128]{1,0:T(8,128)(2,1)S(1)} %get-tuple-element.2), channel_id=4, replica_groups=mesh['delay'=16,'row'=32] {'delay'}, dimensions={0}, use_global_device_ids=true | all-gather | bytes 278528 | tf_op jit(solution)/shard_map/all_gather | solution.py:10
  163.1 0.1 fusion.5
  163.2 0.1 copy.20
  163.3 11.9 %all_to_all.49 = f32[32,2,256]{2,1,0:T(2,128)S(1)} all-to-all(f32[32,2,256]{2,1,0:T(2,128)S(1)} %copy.20), channel_id=1, replica_groups=mesh['delay'=16,'row'=32] {'row'}, dimensions={0} | all-to-all | bytes 131072 | tf_op jit(solution)/shard_map/all_to_all | solution.py:21
  175.2 11.8 %all_to_all.50 = bf16[32,2,256]{2,1,0:T(2,128)(2,1)S(1)} all-to-all(bf16[32,2,256]{2,1,0:T(2,128)(2,1)S(1)} %broadcast_in_dim.24), channel_id=1, replica_groups=mesh['delay'=16,'row'=32] {'row'}, dimensions={0} | all-to-all | bytes 65536 | tf_op jit(solution)/shard_map/all_to_all | solution.py:27
  187.0 0.9 stack.15
  187.8 7.4 %all-to-all-start.8 = ((bf16[16,64,256]{2,1,0:T(8,128)(2,1)}), bf16[16,64,256]{2,1,0:T(8,128)(2,1)S(1)}, u32[]{:S(2)}, u32[]{:S(2)}) async-start(bf16[16,64,256]{2,1,0:T(8,128)(2,1)} %stack.15), calls=%async_computation.8 | async-start | bytes 1048576 | tf_op jit(solution)/shard_map/all_to_all | solution.py:62
  195.3 2.0 collective-permute-start.2
  197.4 0.7 pad_maximum_fusion
  198.0 14.6 %all-to-all-done.8 = bf16[16,64,256]{2,1,0:T(8,128)(2,1)S(1)} async-done(((bf16[16,64,256]{2,1,0:T(8,128)(2,1)}), bf16[16,64,256]{2,1,0:T(8,128)(2,1)S(1)}, u32[]{:S(2)}, u32[]{:S(2)}) %all-to-all-start.8) | async-done | bytes 524320 | tf_op jit(solution)/shard_map/all_to_all | solution.py:62
  212.6 0.3 fusion
  213.0 0.0 collective-permute-done.2
  213.0 0.6 add_bitcast_fusion
  (21 shorter events, 0.5 us)
Async XLA Ops:
  0.6 81.1 %copy-start = (bf16[1,4096,128]{2,1,0:T(8,128)(2,1)S(1)}, bf16[1,4096,128]{2,1,0:T(8,128)(2,1)}, u32[]{:S(2)}) copy-start(bf16[1,4096,128]{2,1,0:T(8,128)(2,1)} %param.10) | copy-start | bytes 3145732
  2.3 21.7 %copy-start.1 = (bf16[128,256]{1,0:T(8,128)(2,1)S(1)}, bf16[128,256]{1,0:T(8,128)(2,1)}, u32[]{:S(2)}) copy-start(bf16[128,256]{1,0:T(8,128)(2,1)} %param.9) | copy-start | bytes 196612
  43.8 0.7 copy-start.4
  57.2 7.2 %copy-start.3 = (f32[1,64,128]{2,1,0:T(8,128)S(1)}, f32[1,64,128]{2,1,0:T(8,128)}, u32[]{:S(2)}) copy-start(f32[1,64,128]{2,1,0:T(8,128)} %param.11) | copy-start | bytes 98308
  57.2 24.5 %all-to-all-start.2 = ((bf16[16,64,256]{2,1,0:T(8,128)(2,1)}), bf16[16,64,256]{2,1,0:T(8,128)(2,1)S(1)}, u32[]{:S(2)}, u32[]{:S(2)}) async-start(bf16[16,64,256]{2,1,0:T(8,128)(2,1)} %stack.12), calls=%async_computation.2 | async-start | bytes 1048576 | tf_op jit(solution)/shard_map/all_to_all | solution.py:62
  64.3 17.4 %collective-permute-start = (f32[64,128]{1,0:T(8,128)S(1)}, f32[64,128]{1,0:T(8,128)S(1)}, u32[]{:S(2)}, u32[]{:S(2)}) collective-permute-start(f32[64,128]{1,0:T(8,128)S(1)} %bitcast.44), channel_id=1, source_target_pairs={{32,0},{64,32},{96,64},{128,96},{160,128},{192,160},{224,192},{256... | collective-permute-start | bytes 98312 | tf_op jit(solution)/shard_map/ppermute | solution.py:44
  81.7 0.7 copy-start.2
  122.7 24.8 %all-to-all-start.5 = ((bf16[16,64,256]{2,1,0:T(8,128)(2,1)}), bf16[16,64,256]{2,1,0:T(8,128)(2,1)S(1)}, u32[]{:S(2)}, u32[]{:S(2)}) async-start(bf16[16,64,256]{2,1,0:T(8,128)(2,1)} %stack.13), calls=%async_computation.5 | async-start | bytes 1048576 | tf_op jit(solution)/shard_map/all_to_all | solution.py:62
  130.1 17.7 %collective-permute-start.1 = (f32[64,128]{1,0:T(8,128)S(1)}, f32[64,128]{1,0:T(8,128)S(1)}, u32[]{:S(2)}, u32[]{:S(2)}) collective-permute-start(f32[64,128]{1,0:T(8,128)S(1)} %get-tuple-element.8), channel_id=1, source_target_pairs={{32,0},{64,32},{96,64},{128,96},{160,128},{192,160},{224,192},{256... | collective-permute-start | bytes 98312 | tf_op jit(solution)/shard_map/ppermute | solution.py:44
  187.8 24.8 %all-to-all-start.8 = ((bf16[16,64,256]{2,1,0:T(8,128)(2,1)}), bf16[16,64,256]{2,1,0:T(8,128)(2,1)S(1)}, u32[]{:S(2)}, u32[]{:S(2)}) async-start(bf16[16,64,256]{2,1,0:T(8,128)(2,1)} %stack.15), calls=%async_computation.8 | async-start | bytes 1048576 | tf_op jit(solution)/shard_map/all_to_all | solution.py:62
  195.3 17.6 %collective-permute-start.2 = (f32[64,128]{1,0:T(8,128)S(1)}, f32[64,128]{1,0:T(8,128)S(1)}, u32[]{:S(2)}, u32[]{:S(2)}) collective-permute-start(f32[64,128]{1,0:T(8,128)S(1)} %get-tuple-element.3), channel_id=1, source_target_pairs={{32,0},{64,32},{96,64},{128,96},{160,128},{192,160},{224,192},{256... | collective-permute-start | bytes 98312 | tf_op jit(solution)/shard_map/ppermute | solution.py:44
